TPU v7x, 32 devices: a whole 2x2x4 slice. The times are simulated.
32 devices in a mesh: dp: 8 (over y, x, core), tensor: 4 (over z).
Axes of the slice: x: 2, y: 2, z: 4, core: 2. Of those that a mesh axis runs over, the one named last changes fastest.
Arguments:
- tokens: bfloat16 [2048, 8192], P('dp'), may hold values from -6 to 6
- router_weight: bfloat16 [8192, 8], replicated, may hold values from -0.0625 to 0.0625
- gate_weight: bfloat16 [14336, 8192], P(('dp', 'tensor')), may hold values from -0.0625 to 0.0625
- up_weight: bfloat16 [14336, 8192], P(('dp', 'tensor')), may hold values from -0.0625 to 0.0625
- down_weight: bfloat16 [14336, 8192], P(('dp', 'tensor')), may hold values from -0.125 to 0.125
- cluster_of: int32 [14336, 1], P('dp'), may hold values from 0 to 7; in each aligned block of 1792 rows (0 to 1791, 1792 to 3583, ...) at most 448 rows name the same one
- expert_ids: int32 [2048, 2], P('dp'), may hold values from 0 to 7, all different within a row; in each aligned block of 256 rows (0 to 255, 256 to 511, ...) at most 128 rows name the same one
Outputs:
- mixed_out: bfloat16 [2048, 8192], P('dp', 'tensor')
Inputs may be any that keep to these rules, and one draw needn't show every extreme that they name: `expert_ids`: in each aligned block of 256 rows (the tokens of one dp index) no expert is named by more than 128 rows, a bound that some block reaches; a row names two different experts; every expert is named somewhere. `cluster_of`: in each aligned block of 1792 hidden units no cluster holds more than 448 units, and some cluster holds exactly 448; every cluster holds some unit.
All inputs are finite; a program needn't handle non-finite values.
Results may differ from a plain program's by a relative error of at most 0.023.
Values may be sent and summed in bfloat16 or wider, within the bound.
A program may use at most 192 MiB of HBM per device.

v0:
```python
import jax
import jax.numpy as jnp
from jax import lax
from jax.sharding import PartitionSpec as P


def place_rows(labels, bin_count, capacity):
    count_rows = labels.shape[0]
    onehot = (labels[:, None] == jnp.arange(bin_count, dtype=jnp.int32)[None, :]).astype(jnp.int32)
    before = jnp.cumsum(onehot, axis=0) - onehot
    rank_in = jnp.sum(before * onehot, axis=1)
    position = labels * capacity + rank_in
    slot_list = jnp.full((bin_count * capacity,), count_rows, jnp.int32)
    slot_list = slot_list.at[position].set(jnp.arange(count_rows, dtype=jnp.int32))
    return (slot_list, position)


def with_zero_row(matrix):
    return jnp.concatenate([matrix, jnp.zeros((1, matrix.shape[1]), matrix.dtype)], axis=0)


def against(left_side, right_side):
    return lax.dot_general(
        left_side, right_side, (((1,), (1,)), ((), ())), preferred_element_type=jnp.float32
    )


def on_device(tokens, router_weight, gate_weight, up_weight, down_weight, cluster_of, expert_ids):
    owners = lax.axis_size("dp")
    tensor_count = lax.axis_size("tensor")
    width_part = tokens.shape[1] // tensor_count
    token_count = tokens.shape[0]
    gate_rows, up_rows, down_rows = (
        lax.all_to_all(gate_weight, "tensor", split_axis=1, concat_axis=0, tiled=True),
        lax.all_to_all(up_weight, "tensor", split_axis=1, concat_axis=0, tiled=True),
        lax.all_to_all(down_weight, "tensor", split_axis=1, concat_axis=0, tiled=True),
    )
    unit_cap = 2 * gate_rows.shape[0] // owners
    unit_list, unit_spot = place_rows(cluster_of[:, 0], owners, unit_cap)
    gate_pick = with_zero_row(gate_rows)[unit_list]
    up_pick = with_zero_row(up_rows)[unit_list]
    down_pick = with_zero_row(down_rows)[unit_list]
    gate_own, up_own, down_own = (
        lax.all_to_all(gate_pick, "dp", split_axis=0, concat_axis=0, tiled=True),
        lax.all_to_all(up_pick, "dp", split_axis=0, concat_axis=0, tiled=True),
        lax.all_to_all(down_pick, "dp", split_axis=0, concat_axis=0, tiled=True),
    )
    capacity = 4 * token_count // owners
    flat_ids = expert_ids.reshape(-1)
    slot_list, slot_spot = place_rows(flat_ids, owners, capacity)
    features = lax.dynamic_slice_in_dim(
        tokens, lax.axis_index("tensor") * width_part, width_part, 1
    )
    outgoing = with_zero_row(features)[slot_list // 2]
    arrived = lax.all_to_all(outgoing, "dp", split_axis=0, concat_axis=0, tiled=True)
    gate_part = against(arrived, gate_own)
    up_part = against(arrived, up_own)
    gate_sum, up_sum = (
        lax.psum(gate_part.astype(jnp.bfloat16), "tensor").astype(jnp.float32),
        lax.psum(up_part.astype(jnp.bfloat16), "tensor").astype(jnp.float32),
    )
    hidden = (jax.nn.silu(gate_sum) * up_sum).astype(jnp.bfloat16)
    expert_out = jnp.dot(hidden, down_own, preferred_element_type=jnp.float32).astype(jnp.bfloat16)
    returned = lax.all_to_all(expert_out, "dp", split_axis=0, concat_axis=0, tiled=True)
    picked_out = returned[slot_spot].reshape(token_count, 2, width_part)
    logits = jnp.dot(tokens, router_weight, preferred_element_type=jnp.float32)
    scores = jax.nn.sigmoid(jnp.take_along_axis(logits, expert_ids, axis=1))
    mixing = scores / jnp.sum(scores, axis=1, keepdims=True)
    mixed_out = jnp.sum(mixing[:, :, None] * picked_out.astype(jnp.float32), axis=1)
    return mixed_out.astype(jnp.bfloat16)


def solution(mesh):
    in_specs = (
        P("dp", None),
        P(),
        P(("dp", "tensor"), None),
        P(("dp", "tensor"), None),
        P(("dp", "tensor"), None),
        P("dp", None),
        P("dp", None),
    )
    out_specs = P("dp", "tensor")
    return jax.shard_map(
        on_device, mesh=mesh, in_specs=in_specs, out_specs=out_specs, check_vma=False
    )
```

profile of v0, /device:TPU:0, one launch (start us, length us, event | category | flops | bytes accessed | tf_op | source)
XLA Modules:
  0.0 1509.2 jit_solution(15491347684281277465)
XLA Ops:
  6.5 0.8 copy.27
  7.4 0.1 eq.54
  7.5 0.1 eq.50
  7.7 0.7 broadcast_multiply_fusion
  8.4 1.1 reduce-window.14
  9.5 0.2 slice_reduce_fusion.1
  9.9 0.1 mul.51
  10.2 2.4 scatter_custom_fusion
  12.7 1.3 constant_dynamic-slice_fusion
  14.1 6.0 gather_fusion
  20.1 5.2 all-to-all-start
  25.3 7.4 copy.41
  32.7 41.8 %all-to-all-done = bf16[8,128,2048]{2,1,0:T(8,128)(2,1)} async-done(((bf16[8,128,2048]{2,1,0:T(8,128)(2,1)}), bf16[8,128,2048]{2,1,0:T(8,128)(2,1)}, u32[]{:S(2)}, u32[]{:S(2)}) %all-to-all-start) | async-done | bytes 4194336 | tf_op jit(solution)/shard_map/all_to_all | solution.py:55
  74.5 5.6 all-to-all-start.3
  80.1 7.5 copy.42
  87.6 151.0 %all-to-all-done.3 = bf16[448,4,2048]{2,0,1:T(8,128)(2,1)} async-done(((bf16[448,4,2048]{2,0,1:T(8,128)(2,1)}), bf16[448,4,2048]{2,0,1:T(8,128)(2,1)}, u32[]{:S(2)}, u32[]{:S(2)}) %all-to-all-start.3) | async-done | bytes 7340064 | tf_op jit(solution)/shard_map/all_to_all | solution.py:35
  238.6 5.6 all-to-all-start.1
  244.2 2.3 reduce-window.16
  246.5 0.3 slice_reduce_fusion
  246.8 0.2 reduce-window.19
  247.2 7.1 scatter_custom_fusion.1
  254.3 7.5 concatenate.14
  261.8 31.6 %gather_fusion.2 = bf16[3584,2048]{1,0:T(8,128)(2,1)} fusion(bf16[1793,2048]{1,0:T(8,128)(2,1)} %concatenate.14, s32[4096]{0:T(1024)S(1)} %pad_clamp_fusion), kind=kCustom, calls=%fused_computation.2 | custom fusion | bytes 29374464 | tf_op jit(solution)/shard_map/gather | solution.py:41
  293.4 110.7 %all-to-all-done.1 = bf16[448,4,2048]{2,0,1:T(8,128)(2,1)} async-done(((bf16[448,4,2048]{2,0,1:T(8,128)(2,1)}), bf16[448,4,2048]{2,0,1:T(8,128)(2,1)}, u32[]{:S(2)}, u32[]{:S(2)}) %all-to-all-start.1) | async-done | bytes 7340064 | tf_op jit(solution)/shard_map/all_to_all | solution.py:34
  404.2 17.4 %all-to-all-start.4 = ((bf16[8,448,2048]{2,1,0:T(8,128)(2,1)}), bf16[8,448,2048]{2,1,0:T(8,128)(2,1)}, u32[]{:S(2)}, u32[]{:S(2)}) async-start(bf16[8,448,2048]{2,1,0:T(8,128)(2,1)} %bitcast.72), calls=%async_computation.4 | async-start | bytes 29360128 | tf_op jit(solution)/shard_map/all_to_all | solution.py:45
  421.6 7.5 concatenate.13
  429.1 31.7 %gather_fusion.1 = bf16[3584,2048]{1,0:T(8,128)(2,1)} fusion(bf16[1793,2048]{1,0:T(8,128)(2,1)} %concatenate.13, s32[4096]{0:T(1024)S(1)} %pad_clamp_fusion), kind=kCustom, calls=%fused_computation.1 | custom fusion | bytes 29374464 | tf_op jit(solution)/shard_map/gather | solution.py:40
  460.8 122.2 %all-to-all-done.4 = bf16[8,448,2048]{2,1,0:T(8,128)(2,1)} async-done(((bf16[8,448,2048]{2,1,0:T(8,128)(2,1)}), bf16[8,448,2048]{2,1,0:T(8,128)(2,1)}, u32[]{:S(2)}, u32[]{:S(2)}) %all-to-all-start.4) | async-done | bytes 14680096 | tf_op jit(solution)/shard_map/all_to_all | solution.py:45
  582.9 5.5 all-to-all-start.2
  588.5 7.5 copy.40
  595.9 154.0 %all-to-all-done.2 = bf16[8,448,2048]{2,1,0:T(8,128)(2,1)} async-done(((bf16[8,448,2048]{2,1,0:T(8,128)(2,1)}), bf16[8,448,2048]{2,1,0:T(8,128)(2,1)}, u32[]{:S(2)}, u32[]{:S(2)}) %all-to-all-start.2) | async-done | bytes 14680096 | tf_op jit(solution)/shard_map/all_to_all | solution.py:44
  749.9 5.4 all-to-all-start.5
  755.4 21.7 %convolution_convert_fusion = bf16[1024,3584]{1,0:T(8,128)(2,1)} fusion(bf16[1024,2048]{1,0:T(8,128)(2,1)} %bitcast.6, bf16[3584,2048]{1,0:T(8,128)(2,1)} %bitcast.15), kind=kOutput, calls=%fused_computation.15 | convolution fusion | flops 15036055552 | bytes 26214400 | tf_op jit(solution)/shard_map/dot_general | solution.py:23
  777.2 22.2 %convolution_convert_fusion.1 = bf16[1024,3584]{1,0:T(8,128)(2,1)} fusion(bf16[1024,2048]{1,0:T(8,128)(2,1)} %bitcast.6, bf16[3584,2048]{1,0:T(8,128)(2,1)} %bitcast.11), kind=kOutput, calls=%fused_computation.16 | convolution fusion | flops 15036055552 | bytes 26214400 | tf_op jit(solution)/shard_map/dot_general | solution.py:23
  799.4 250.4 %all-to-all-done.5 = bf16[448,4,2048]{2,0,1:T(8,128)(2,1)} async-done(((bf16[448,4,2048]{2,0,1:T(8,128)(2,1)}), bf16[448,4,2048]{2,0,1:T(8,128)(2,1)}, u32[]{:S(2)}, u32[]{:S(2)}) %all-to-all-start.5) | async-done | bytes 7340064 | tf_op jit(solution)/shard_map/all_to_all | solution.py:36
  1049.8 7.4 concatenate.15
  1057.3 31.6 %gather_fusion.3 = bf16[3584,2048]{1,0:T(8,128)(2,1)} fusion(bf16[1793,2048]{1,0:T(8,128)(2,1)} %concatenate.15, s32[4096]{0:T(1024)S(1)} %pad_clamp_fusion), kind=kCustom, calls=%fused_computation.3 | custom fusion | bytes 29374464 | tf_op jit(solution)/shard_map/gather | solution.py:42
  1088.9 168.8 %all_to_all.117 = bf16[8,448,2048]{2,1,0:T(8,128)(2,1)} all-to-all(bf16[8,448,2048]{2,1,0:T(8,128)(2,1)} %bitcast.74), channel_id=1, replica_groups=mesh['dp'=8,'tensor'=4] {'dp'}, dimensions={0} | all-to-all | bytes 29360128 | tf_op jit(solution)/shard_map/all_to_all | solution.py:46
  1257.7 144.9 %all-reduce.7.cloned.1.call-done = (bf16[1024,3584]{1,0:T(8,128)(2,1)}, bf16[1024,3584]{1,0:T(8,128)(2,1)}) async-done(((bf16[1024,3584]{1,0:T(8,128)(2,1)}, bf16[1024,3584]{1,0:T(8,128)(2,1)}), (bf16[1024,3584]{1,0:T(8,128)(2,1)}, bf16[1024,3584]{1,0:T(8,128)(2,1)})) %all-reduce.7.cloned.1.call-update) | async-done | bytes 14680080 | tf_op jit(solution)/shard_map/psum | solution.py:60
  1402.6 24.6 %fusion.7 = bf16[1024,2048]{1,0:T(8,128)(2,1)} fusion(bf16[3584,2048]{1,0:T(8,128)(2,1)} %bitcast.79, bf16[1024,3584]{1,0:T(8,128)(2,1)} %get-tuple-element.5, bf16[1024,3584]{1,0:T(8,128)(2,1)} %get-tuple-element.6), kind=kOutput, calls=%fused_computation.22 | convolution fusion | flops 15063842816 | bytes 33554432 | tf_op jit(solution)/shard_map/dot_general | solution.py:63
  1427.2 4.8 all-to-all-start.7
  1432.2 0.1 reshape.153
  1432.4 3.4 fusion.27
  1435.7 3.5 gather_fusion.5
  1439.7 41.5 %all-to-all-done.7 = bf16[8,128,2048]{2,1,0:T(8,128)(2,1)} async-done(((bf16[8,128,2048]{2,1,0:T(8,128)(2,1)}), bf16[8,128,2048]{2,1,0:T(8,128)(2,1)}, u32[]{:S(2)}, u32[]{:S(2)}) %all-to-all-start.7) | async-done | bytes 4194336 | tf_op jit(solution)/shard_map/all_to_all | solution.py:64
  1481.2 7.1 gather_fusion.4
  1488.3 4.0 reshape.112
  1492.3 9.9 multiply_reduce_fusion
  (37 shorter events, 1.2 us)
Async XLA Ops:
  6.5 1425.8 %copy-start = (bf16[8192,8]{0,1:T(8,128)(2,1)S(1)}, bf16[8192,8]{0,1:T(8,128)(2,1)}, u32[]{:S(2)}) copy-start(bf16[8192,8]{0,1:T(8,128)(2,1)} %param.8) | copy-start | bytes 393220
  10.2 2.5 copy-start.3
  20.1 54.4 %all-to-all-start = ((bf16[8,128,2048]{2,1,0:T(8,128)(2,1)}), bf16[8,128,2048]{2,1,0:T(8,128)(2,1)}, u32[]{:S(2)}, u32[]{:S(2)}) async-start(bf16[8,128,2048]{2,1,0:T(8,128)(2,1)} %bitcast.78), calls=%async_computation | async-start | bytes 8388608 | tf_op jit(solution)/shard_map/all_to_all | solution.py:55
  74.5 164.1 %all-to-all-start.3 = ((bf16[448,4,2048]{2,0,1:T(8,128)(2,1)}), bf16[448,4,2048]{2,0,1:T(8,128)(2,1)}, u32[]{:S(2)}, u32[]{:S(2)}) async-start(bf16[448,4,2048]{2,0,1:T(8,128)(2,1)} %bitcast.77), calls=%async_computation.3 | async-start | bytes 14680064 | tf_op jit(solution)/shard_map/all_to_all | solution.py:35
  238.6 5.6 copy-start.2
  238.6 165.6 %all-to-all-start.1 = ((bf16[448,4,2048]{2,0,1:T(8,128)(2,1)}), bf16[448,4,2048]{2,0,1:T(8,128)(2,1)}, u32[]{:S(2)}, u32[]{:S(2)}) async-start(bf16[448,4,2048]{2,0,1:T(8,128)(2,1)} %bitcast.75), calls=%async_computation.1 | async-start | bytes 14680064 | tf_op jit(solution)/shard_map/all_to_all | solution.py:34
  404.2 178.7 %all-to-all-start.4 = ((bf16[8,448,2048]{2,1,0:T(8,128)(2,1)}), bf16[8,448,2048]{2,1,0:T(8,128)(2,1)}, u32[]{:S(2)}, u32[]{:S(2)}) async-start(bf16[8,448,2048]{2,1,0:T(8,128)(2,1)} %bitcast.72), calls=%async_computation.4 | async-start | bytes 29360128 | tf_op jit(solution)/shard_map/all_to_all | solution.py:45
  582.9 167.0 %all-to-all-start.2 = ((bf16[8,448,2048]{2,1,0:T(8,128)(2,1)}), bf16[8,448,2048]{2,1,0:T(8,128)(2,1)}, u32[]{:S(2)}, u32[]{:S(2)}) async-start(bf16[8,448,2048]{2,1,0:T(8,128)(2,1)} %bitcast.73), calls=%async_computation.2 | async-start | bytes 29360128 | tf_op jit(solution)/shard_map/all_to_all | solution.py:44
  749.9 299.9 %all-to-all-start.5 = ((bf16[448,4,2048]{2,0,1:T(8,128)(2,1)}), bf16[448,4,2048]{2,0,1:T(8,128)(2,1)}, u32[]{:S(2)}, u32[]{:S(2)}) async-start(bf16[448,4,2048]{2,0,1:T(8,128)(2,1)} %bitcast.76), calls=%async_computation.5 | async-start | bytes 14680064 | tf_op jit(solution)/shard_map/all_to_all | solution.py:36
  755.4 647.2 %all-reduce.7.cloned.1.call-start = ((), (), s32[]{:S(2)}) async-start(), calls=%async_computation.8 | async-start | bytes 29360128 | tf_op jit(solution)/shard_map/psum | solution.py:60
  1427.2 4.9 copy-start.1
  1427.2 54.0 %all-to-all-start.7 = ((bf16[8,128,2048]{2,1,0:T(8,128)(2,1)}), bf16[8,128,2048]{2,1,0:T(8,128)(2,1)}, u32[]{:S(2)}, u32[]{:S(2)}) async-start(bf16[8,128,2048]{2,1,0:T(8,128)(2,1)} %bitcast.83), calls=%async_computation.7 | async-start | bytes 8388608 | tf_op jit(solution)/shard_map/all_to_all | solution.py:64
  1435.7 3.9 copy-start.4
Sparse Core Ops, SparseCore 0:
  799.5 603.0 all-reduce.6
where the time goes:
time: 1520 us; the launch traced here: 1510 us
  waiting for transfers between devices  1020 us (67%)
  local copies, waits for them, and re-layouts  174 us (11%)
  blocking collectives  169 us (11%)
  matrix products  71.9 us (5%)
  starting transfers between devices  49.6 us (3%)
    all_to_all x1, waiting for transfers between devices, on_device(): lax.all_to_all(down_weight, 'tensor', split_axis=1, concat_axis=0, tiled=...  250 us
    all_to_all x1, blocking collectives, on_device(): lax.all_to_all(down_pick, 'dp', split_axis=0, concat_axis=0, tiled=True)  169 us
    all_to_all x1, waiting for transfers between devices, on_device(): lax.all_to_all(gate_pick, 'dp', split_axis=0, concat_axis=0, tiled=True)  154 us
    all_to_all x1, waiting for transfers between devices, on_device(): lax.all_to_all(up_weight, 'tensor', split_axis=1, concat_axis=0, tiled=True)  151 us
    psum x1, waiting for transfers between devices, on_device(): lax.psum(up_part.astype(jnp.bfloat16), 'tensor').astype(jnp.float32)  145 us
    all_to_all x1, waiting for transfers between devices, on_device(): lax.all_to_all(up_pick, 'dp', split_axis=0, concat_axis=0, tiled=True)  122 us
    all_to_all x1, waiting for transfers between devices, on_device(): lax.all_to_all(gate_weight, 'tensor', split_axis=1, concat_axis=0, tiled=...  111 us
    dot_general x2, matrix products, against(): lax.dot_general(left_side, right_side, (((1,), (1,)), ((), ())), preferre...  43.9 us
  transfers between devices with their start and end apart: 8, of which 8 were waited for; matrix products, arithmetic and copies ran while one was open for 13% of the time, Pallas kernels for 0%

commit v1 on v0

v1 whole, which is shorter than its diff:
```python
import jax
import jax.numpy as jnp
from jax import lax
from jax.sharding import PartitionSpec as P

CHUNK_TOKENS = 512


def against(left_side, right_side):
    return lax.dot_general(
        left_side, right_side, (((1,), (1,)), ((), ())), preferred_element_type=jnp.float32
    )


def on_device(tokens, router_weight, gate_weight, up_weight, down_weight, cluster_of, expert_ids):
    owners = lax.axis_size("dp")
    experts = router_weight.shape[1]
    units = gate_weight.shape[0]
    token_count = tokens.shape[0]
    same_core = [list(range(core, owners, 2)) for core in range(2)]
    swap = [(i, i ^ 1) for i in range(owners)]

    own_cluster = lax.dynamic_slice_in_dim(
        cluster_of[:, 0], lax.axis_index("tensor") * units, units, 0
    ).astype(jnp.float32)
    cluster = jnp.concatenate([own_cluster, lax.ppermute(own_cluster, "dp", swap)])
    gate_peer = lax.ppermute(gate_weight, "dp", swap)
    up_peer = lax.ppermute(up_weight, "dp", swap)
    down_peer = lax.ppermute(down_weight, "dp", swap)

    expert_range = jnp.arange(experts, dtype=jnp.int32)
    logits = jnp.dot(tokens, router_weight, preferred_element_type=jnp.float32)
    scores = jax.nn.sigmoid(jnp.take_along_axis(logits, expert_ids, axis=1))
    mixing = scores / jnp.sum(scores, axis=1, keepdims=True)
    shares = jnp.sum(
        jnp.where(expert_ids[:, :, None] == expert_range, mixing[:, :, None], 0.0), axis=1
    )
    unit_onehot = (cluster[None, :] == expert_range.astype(jnp.float32)[:, None]).astype(jnp.float32)

    chunk_count = max(1, token_count * (owners // 2) // CHUNK_TOKENS)
    rows = token_count // chunk_count
    results = []
    down_all = jnp.concatenate([down_weight, down_peer], axis=0)
    for chunk in range(chunk_count):
        piece = tokens[chunk * rows:(chunk + 1) * rows]
        share = shares[chunk * rows:(chunk + 1) * rows]
        if chunk >= 2:
            piece, share, results[-2] = lax.optimization_barrier((piece, share, results[-2]))
        gathered = lax.all_gather(piece, "dp", axis_index_groups=same_core, tiled=True)
        share_all = lax.all_gather(share, "dp", axis_index_groups=same_core, tiled=True)
        scale = jnp.dot(share_all, unit_onehot, precision=lax.Precision.HIGHEST)
        halves = []
        for part, (gate, up) in enumerate(((gate_weight, up_weight), (gate_peer, up_peer))):
            hidden = jax.nn.silu(against(gathered, gate)) * against(gathered, up)
            hidden = hidden * scale[:, part * units:(part + 1) * units]
            halves.append(hidden.astype(jnp.bfloat16))
        hidden = jnp.concatenate(halves, axis=1)
        partial = jnp.dot(hidden, down_all, preferred_element_type=jnp.float32).astype(jnp.bfloat16)
        summed = lax.psum_scatter(
            partial, "dp", scatter_dimension=0, axis_index_groups=same_core, tiled=True
        )
        results.append(lax.psum_scatter(summed, "tensor", scatter_dimension=1, tiled=True))
    return jnp.concatenate(results, axis=0)


def solution(mesh):
    in_specs = (
        P("dp", None),
        P(),
        P(("dp", "tensor"), None),
        P(("dp", "tensor"), None),
        P(("dp", "tensor"), None),
        P("dp", None),
        P("dp", None),
    )
    return jax.shard_map(
        on_device, mesh=mesh, in_specs=in_specs, out_specs=P("dp", "tensor"), check_vma=False
    )
```

time: 1520 us -> 472 us (0.31)
  waiting for transfers between devices: 1020 us -> 322 us
  blocking collectives: 169 us -> 17.7 us
  local copies, waits for them, and re-layouts: 174 us -> 23.4 us
  starting transfers between devices: 49.6 us -> 1.75 us
  matrix products: 71.9 us -> 89.5 us
    all_to_all x7 -> x0, waiting for transfers between devices: 872 us -> none  [the longest x1 250 us: on_device(): lax.all_to_all(down_weight, 'tensor', split_axis=1, concat_axis=0, tiled=...]
    reduce_scatter x0 -> x4, waiting for transfers between devices: none -> 230 us  [the longest x2 138 us: on_device(): lax.psum_scatter(partial, 'dp', scatter_dimension=0, axis_index_groups=sa...]
    all_to_all x1 -> x0, blocking collectives: 169 us -> none  [on_device(): lax.all_to_all(down_pick, 'dp', split_axis=0, concat_axis=0, tiled=True)]
    psum x1 -> x0, waiting for transfers between devices: 145 us -> none  [on_device(): lax.psum(up_part.astype(jnp.bfloat16), 'tensor').astype(jnp.float32)]
    gather x5 -> x0, local copies, waits for them, and re-layouts: 108 us -> none  [the longest x1 31.7 us: on_device(): gate_pick = with_zero_row(gate_rows)[unit_list]]
    all_gather x0 -> x2, waiting for transfers between devices: none -> 91.6 us  [on_device(): lax.all_gather(piece, 'dp', axis_index_groups=same_core, tiled=True)]
    all_to_all x7 -> x0, starting transfers between devices: 49.6 us -> none  [the longest x1 17.4 us: on_device(): lax.all_to_all(up_pick, 'dp', split_axis=0, concat_axis=0, tiled=True)]
    all_to_all x3 -> x0, local copies, waits for them, and re-layouts: 22.4 us -> none  [the longest x1 7.49 us: on_device(): lax.all_to_all(gate_weight, 'tensor', split_axis=1, concat_axis=0, tiled=...]
  transfers between devices with their start and end apart: 8 -> 10, of which waited for: 8 -> 6; matrix products, arithmetic and copies ran while one was open for 13% -> 23% of each run, Pallas kernels for 0% -> 0%
where the time goes in v1:
time: 472 us; the launch traced here: 471 us
  waiting for transfers between devices  322 us (68%)
  matrix products  89.5 us (19%)
  local copies, waits for them, and re-layouts  23.4 us (5%)
  blocking collectives  17.7 us (4%)
  between operations  13.8 us (3%)
    reduce_scatter x2, waiting for transfers between devices, on_device(): lax.psum_scatter(partial, 'dp', scatter_dimension=0, axis_index_groups=sa...  138 us
    all_gather x2, waiting for transfers between devices, on_device(): lax.all_gather(piece, 'dp', axis_index_groups=same_core, tiled=True)  91.6 us
    reduce_scatter x2, waiting for transfers between devices, on_device(): lax.psum_scatter(summed, 'tensor', scatter_dimension=1, tiled=True)  91.5 us
    dot_general x8, matrix products, against(): lax.dot_general(left_side, right_side, (((1,), (1,)), ((), ())), preferre...  60.5 us
    dot_general x2, matrix products, on_device(): jnp.dot(hidden, down_all, preferred_element_type=jnp.float32)  23.7 us
    all_gather x2, blocking collectives, on_device(): lax.all_gather(share, 'dp', axis_index_groups=same_core, tiled=True)  17.7 us
  transfers between devices with their start and end apart: 10, of which 6 were waited for; matrix products, arithmetic and copies ran while one was open for 23% of the time, Pallas kernels for 0%

profile of v1, /device:TPU:0, one launch (start us, length us, event | category | flops | bytes accessed | tf_op | source)
XLA Modules:
  0.0 471.3 jit_solution(11419903908160675521)
XLA Ops:
  6.5 4.7 fusion.23
  11.2 0.0 all-gather.3.cloned.1.call-update
  11.2 0.0 all-gather.5.cloned.1.call-start
  11.3 0.5 collective-permute-start.3
  11.8 0.2 all-gather.5.cloned.1.call-update
  12.0 0.0 reduce-scatter.5.cloned.1.call-start
  12.0 0.5 collective-permute-start.1
  12.5 0.8 dynamic-slice_convert_fusion
  13.3 0.1 collective-permute-start
  13.4 0.5 collective-permute-start.2
  13.8 0.1 copy.34
  14.0 0.1 reshape.33
  14.1 3.4 fusion.26
  17.5 3.5 gather_fusion
  21.0 0.1 reshape.36
  21.2 0.1 copy.35
  21.3 7.8 %constant_dynamic-update-slice_fusion.1 = bf16[896,8192]{1,0:T(8,128)(2,1)} fusion(bf16[448,8192]{1,0:T(8,128)(2,1)} %param.11), kind=kLoop, calls=%fused_computation.32 | loop fusion | bytes 14680064
  29.1 9.4 %all_gather.13 = f32[512,8]{0,1:T(8,128)S(1)} all-gather(f32[128,8]{0,1:T(8,128)S(1)} %get-tuple-element.9), channel_id=1, replica_groups={{0,8,16,24},{4,12,20,28},{1,9,17,25},{5,13,21,29},{2,10,18,26},{6,14,22..., dimensions={0}, use_global_device_ids=true | all-gather | bytes 20480 | tf_op jit(solution)/shard_map/all_gather | solution.py:50
  38.5 0.1 pad_maximum_fusion.1
  38.6 1.0 fusion.14
  39.6 6.9 %constant_dynamic-update-slice_fusion = bf16[896,8192]{1,0:T(8,128)(2,1)} fusion(bf16[896,8192]{1,0:T(8,128)(2,1)} %constant_dynamic-update-slice_fusion.1, bf16[448,8192]{1,0:T(8,128)(2,1)} %collective-permute-done.3), kind=kLoop, calls=%fused_computation.31 | loop fusion | bytes 14680064 | tf_op jit(solution)/shard_map/concatenate | solution.py:43
  46.5 55.3 %all-gather.3.cloned.1.call-done = bf16[512,8192]{1,0:T(8,128)(2,1)} async-done(((bf16[128,8192]{1,0:T(8,128)(2,1)}), bf16[512,8192]{1,0:T(8,128)(2,1)}) %all-gather.3.cloned.1.call-update) | async-done | bytes 8388624 | tf_op jit(solution)/shard_map/all_gather | solution.py:49
  101.8 8.8 %fusion.25 = f32[512,448]{0,1:T(8,128)S(1)} fusion(bf16[512,8192]{1,0:T(8,128)(2,1)} %all-gather.3.cloned.1.call-done, bf16[448,8192]{1,0:T(8,128)(2,1)} %param.9), kind=kOutput, calls=%fused_computation.46 | convolution fusion | flops 3758096384 | bytes 16646144 | tf_op jit(solution)/shard_map/dot_general | solution.py:10
  110.6 8.1 %fusion.27 = f32[512,448]{0,1:T(8,128)S(1)} fusion(bf16[512,8192]{1,0:T(8,128)(2,1)S(1)} %copy-done.4, bf16[448,8192]{1,0:T(8,128)(2,1)} %collective-permute-done.1), kind=kOutput, calls=%fused_computation.48 | convolution fusion | flops 3758096384 | bytes 16646144 | tf_op jit(solution)/shard_map/dot_general | solution.py:10
  118.7 7.5 %fusion.3 = bf16[512,448]{0,1:T(8,128)(2,1)S(1)} fusion(bf16[512,8192]{1,0:T(8,128)(2,1)S(1)} %copy-done.4, bf16[448,8192]{1,0:T(8,128)(2,1)} %param.10, f32[512,896]{0,1:T(8,128)S(1)} %fusion.14, f32[512,448]{0,1:T(8,128)S(1)} %fusion.25), kind=kOutput, calls=%fused_computation.8 | convolution fusion | flops 3759702016 | bytes 18022400 | tf_op jit(solution)/shard_map/dot_general | solution.py:10
  126.2 7.5 %fusion.5 = bf16[512,448]{0,1:T(8,128)(2,1)S(1)} fusion(f32[512,896]{0,1:T(8,128)S(1)} %fusion.14, f32[512,448]{0,1:T(8,128)S(1)} %fusion.27, bf16[512,8192]{1,0:T(8,128)(2,1)S(1)} %copy-done.4, bf16[448,8192]{1,0:T(8,128)(2,1)} %collective-permute-done.2), kind=kOutput, calls=%fused_computation.13 | convolution fusion | flops 3759702016 | bytes 18022400 | tf_op jit(solution)/shard_map/dot_general | solution.py:10
  133.8 11.9 %convolution_convert_fusion.1 = bf16[512,8192]{1,0:T(8,128)(2,1)} fusion(bf16[896,8192]{1,0:T(8,128)(2,1)S(1)} %bitcast.28, bf16[512,448]{0,1:T(8,128)(2,1)S(1)} %fusion.5, bf16[512,448]{0,1:T(8,128)(2,1)S(1)} %fusion.3), kind=kOutput, calls=%fused_computation.2 | convolution fusion | flops 7522222080 | bytes 23986176 | tf_op jit(solution)/shard_map/dot_general | solution.py:58
  145.7 0.0 reduce-scatter.5.cloned.1.call-update
  145.7 0.0 reduce-scatter.9.cloned.1.call-start
  145.8 8.3 %all_gather.15 = f32[512,8]{0,1:T(8,128)S(1)} all-gather(f32[128,8]{0,1:T(8,128)S(1)} %get-tuple-element.10), channel_id=1, replica_groups={{0,8,16,24},{4,12,20,28},{1,9,17,25},{5,13,21,29},{2,10,18,26},{6,14,22..., dimensions={0}, use_global_device_ids=true | all-gather | bytes 20480 | tf_op jit(solution)/shard_map/all_gather | solution.py:50
  154.1 1.0 fusion.12
  155.1 36.4 %all-gather.5.cloned.1.call-done = bf16[512,8192]{1,0:T(8,128)(2,1)} async-done(((bf16[128,8192]{1,0:T(8,128)(2,1)}), bf16[512,8192]{1,0:T(8,128)(2,1)}) %all-gather.5.cloned.1.call-update) | async-done | bytes 8388624 | tf_op jit(solution)/shard_map/all_gather | solution.py:49
  191.4 8.8 %fusion.28 = f32[512,448]{0,1:T(8,128)S(1)} fusion(bf16[512,8192]{1,0:T(8,128)(2,1)} %all-gather.5.cloned.1.call-done, bf16[448,8192]{1,0:T(8,128)(2,1)} %param.9), kind=kOutput, calls=%fused_computation.49 | convolution fusion | flops 3758096384 | bytes 16646144 | tf_op jit(solution)/shard_map/dot_general | solution.py:10
  200.2 0.0 slice-start.9
  200.2 8.1 %fusion.29 = f32[512,448]{0,1:T(8,128)S(1)} fusion(bf16[512,8192]{1,0:T(8,128)(2,1)S(1)} %copy-done.3, bf16[448,8192]{1,0:T(8,128)(2,1)} %collective-permute-done.1), kind=kOutput, calls=%fused_computation.50 | convolution fusion | flops 3758096384 | bytes 16646144 | tf_op jit(solution)/shard_map/dot_general | solution.py:10
  208.4 4.1 fusion.2
  212.5 7.7 %fusion.4 = bf16[512,448]{0,1:T(8,128)(2,1)S(1)} fusion(f32[512,896]{0,1:T(8,128)S(1)} %fusion.12, f32[512,448]{0,1:T(8,128)S(1)} %fusion.29, bf16[512,8192]{1,0:T(8,128)(2,1)S(1)} %copy-done.3, bf16[448,8192]{1,0:T(8,128)(2,1)} %collective-permute-done.2), kind=kOutput, calls=%fused_computation.11 | convolution fusion | flops 3759702016 | bytes 18022400 | tf_op jit(solution)/shard_map/dot_general | solution.py:10
  220.3 11.8 %convolution_convert_fusion = bf16[512,8192]{1,0:T(8,128)(2,1)} fusion(bf16[896,8192]{1,0:T(8,128)(2,1)S(1)} %bitcast.30, bf16[512,448]{0,1:T(8,128)(2,1)S(1)} %fusion.4, bf16[512,448]{0,1:T(8,128)(2,1)S(1)} %fusion.2), kind=kOutput, calls=%fused_computation.1 | convolution fusion | flops 7522222080 | bytes 23986176 | tf_op jit(solution)/shard_map/dot_general | solution.py:58
  232.0 0.0 reduce-scatter.9.cloned.1.call-update
  232.1 0.0 reduce-scatter.7.cloned.1.call-start
  232.1 48.9 %reduce-scatter.5.cloned.1.call-done = bf16[128,8192]{1,0:T(8,128)(2,1)} async-done(((bf16[512,8192]{1,0:T(8,128)(2,1)}), bf16[128,8192]{1,0:T(8,128)(2,1)}) %reduce-scatter.5.cloned.1.call-update) | async-done | bytes 2097168 | tf_op jit(solution)/shard_map/reduce_scatter | solution.py:59
  281.0 0.0 reduce-scatter.7.cloned.1.call-update
  281.0 0.0 reduce-scatter.11.cloned.1.call-start
  281.0 89.6 %reduce-scatter.9.cloned.1.call-done = bf16[128,8192]{1,0:T(8,128)(2,1)} async-done(((bf16[512,8192]{1,0:T(8,128)(2,1)}), bf16[128,8192]{1,0:T(8,128)(2,1)}) %reduce-scatter.9.cloned.1.call-update) | async-done | bytes 2097168 | tf_op jit(solution)/shard_map/reduce_scatter | solution.py:59
  370.6 0.0 reduce-scatter.11.cloned.1.call-update
  370.7 46.0 %reduce-scatter.7.cloned.1.call-done = bf16[128,2048]{1,0:T(8,128)(2,1)} async-done(((bf16[128,8192]{1,0:T(8,128)(2,1)}), bf16[128,2048]{1,0:T(8,128)(2,1)}) %reduce-scatter.7.cloned.1.call-update) | async-done | bytes 524304 | tf_op jit(solution)/shard_map/reduce_scatter | solution.py:62
  416.7 45.5 %reduce-scatter.11.cloned.1.call-done = bf16[128,2048]{1,0:T(8,128)(2,1)} async-done(((bf16[128,8192]{1,0:T(8,128)(2,1)}), bf16[128,2048]{1,0:T(8,128)(2,1)}) %reduce-scatter.11.cloned.1.call-update) | async-done | bytes 524304 | tf_op jit(solution)/shard_map/reduce_scatter | solution.py:62
  462.2 2.3 pad_maximum_fusion
  (43 shorter events, 0.1 us)
Async XLA Ops:
  6.5 7.6 %copy-start = (bf16[8192,8]{0,1:T(8,128)(2,1)S(1)}, bf16[8192,8]{0,1:T(8,128)(2,1)}, u32[]{:S(2)}) copy-start(bf16[8192,8]{0,1:T(8,128)(2,1)} %param.8) | copy-start | bytes 393220
  6.5 7.3 %copy-start.2 = (s32[256,2]{0,1:T(2,128)S(1)}, s32[256,2]{0,1:T(2,128)}, u32[]{:S(2)}) copy-start(s32[256,2]{0,1:T(2,128)} %param.13) | copy-start | bytes 6148
  6.5 95.2 %all-gather.3.cloned.1.call-start = ((), (), s32[]{:S(2)}) async-start(), calls=%async_computation.4 | async-start | bytes 10485760 | tf_op jit(solution)/shard_map/all_gather | solution.py:49
  11.2 180.2 %all-gather.5.cloned.1.call-start = ((), (), s32[]{:S(2)}) async-start(), calls=%async_computation.7 | async-start | bytes 10485760 | tf_op jit(solution)/shard_map/all_gather | solution.py:49
  11.3 28.3 %collective-permute-start.3 = (bf16[448,8192]{1,0:T(8,128)(2,1)}, bf16[448,8192]{1,0:T(8,128)(2,1)}, u32[]{:S(2)}, u32[]{:S(2)}) collective-permute-start(bf16[448,8192]{1,0:T(8,128)(2,1)} %param.11), channel_id=1, source_target_pairs={{0,4},{4,0},{8,12},{12,8},{16,20},{20,16},{24,28},{28,24},{1,5},{5... | collective-permute-start | bytes 22020104 | tf_op jit(solution)/shard_map/ppermute | solution.py:29
  12.0 269.0 %reduce-scatter.5.cloned.1.call-start = ((), (), s32[]{:S(2)}) async-start(), calls=%async_computation.5 | async-start | bytes 10485760 | tf_op jit(solution)/shard_map/reduce_scatter | solution.py:59
  12.0 98.5 %collective-permute-start.1 = (bf16[448,8192]{1,0:T(8,128)(2,1)}, bf16[448,8192]{1,0:T(8,128)(2,1)}, u32[]{:S(2)}, u32[]{:S(2)}) collective-permute-start(bf16[448,8192]{1,0:T(8,128)(2,1)} %param.9), channel_id=1, source_target_pairs={{0,4},{4,0},{8,12},{12,8},{16,20},{20,16},{24,28},{28,24},{1,5},{5... | collective-permute-start | bytes 22020104 | tf_op jit(solution)/shard_map/ppermute | solution.py:27
  13.3 25.2 %collective-permute-start = (f32[448]{0:T(512)S(1)}, f32[448]{0:T(512)S(1)}, u32[]{:S(2)}, u32[]{:S(2)}) collective-permute-start(f32[448]{0:T(512)S(1)} %bitcast.31), channel_id=1, source_target_pairs={{0,4},{4,0},{8,12},{12,8},{16,20},{20,16},{24,28},{28,24},{1,5},{5... | collective-permute-start | bytes 5384 | tf_op jit(solution)/shard_map/ppermute | solution.py:26
  13.4 112.9 %collective-permute-start.2 = (bf16[448,8192]{1,0:T(8,128)(2,1)}, bf16[448,8192]{1,0:T(8,128)(2,1)}, u32[]{:S(2)}, u32[]{:S(2)}) collective-permute-start(bf16[448,8192]{1,0:T(8,128)(2,1)} %param.10), channel_id=1, source_target_pairs={{0,4},{4,0},{8,12},{12,8},{16,20},{20,16},{24,28},{28,24},{1,5},{5... | collective-permute-start | bytes 22020104 | tf_op jit(solution)/shard_map/ppermute | solution.py:28
  101.8 8.8 %copy-start.4 = (bf16[512,8192]{1,0:T(8,128)(2,1)S(1)}, bf16[512,8192]{1,0:T(8,128)(2,1)}, u32[]{:S(2)}) copy-start(bf16[512,8192]{1,0:T(8,128)(2,1)} %all-gather.3.cloned.1.call-done) | copy-start | bytes 25165828
  118.7 15.0 %slice-start = ((s8[14680064]{0:T(1024)(128)(4,1)}), s8[4194304]{0:T(1024)(128)(4,1)S(1)}, s32[]{:S(2)}) async-start(s8[14680064]{0:T(1024)(128)(4,1)} %bitcast.27), calls=%async_computation.10 | async-start | bytes 8388608
  118.7 15.0 %slice-start.1 = ((s8[14680064]{0:T(1024)(128)(4,1)}), s8[4194304]{0:T(1024)(128)(4,1)S(1)}, s32[]{:S(2)}) async-start(s8[14680064]{0:T(1024)(128)(4,1)} %bitcast.27), calls=%async_computation.11 | async-start | bytes 8388608
  126.2 7.5 %slice-start.2 = ((s8[14680064]{0:T(1024)(128)(4,1)}), s8[4194304]{0:T(1024)(128)(4,1)S(1)}, s32[]{:S(2)}) async-start(s8[14680064]{0:T(1024)(128)(4,1)} %bitcast.27), calls=%async_computation.12 | async-start | bytes 8388608
  126.2 7.5 %slice-start.3 = ((s8[14680064]{0:T(1024)(128)(4,1)}), s8[2097152]{0:T(1024)(128)(4,1)S(1)}, s32[]{:S(2)}) async-start(s8[14680064]{0:T(1024)(128)(4,1)} %bitcast.27), calls=%async_computation.13 | async-start | bytes 4194304
  145.7 224.9 %reduce-scatter.9.cloned.1.call-start = ((), (), s32[]{:S(2)}) async-start(), calls=%async_computation.8 | async-start | bytes 10485760 | tf_op jit(solution)/shard_map/reduce_scatter | solution.py:59
  191.4 8.8 %copy-start.3 = (bf16[512,8192]{1,0:T(8,128)(2,1)S(1)}, bf16[512,8192]{1,0:T(8,128)(2,1)}, u32[]{:S(2)}) copy-start(bf16[512,8192]{1,0:T(8,128)(2,1)} %all-gather.5.cloned.1.call-done) | copy-start | bytes 25165828
  191.4 16.9 %slice-start.8 = ((s8[7340032]{0:T(1024)(128)(4,1)}), s8[4194304]{0:T(1024)(128)(4,1)S(1)}, s32[]{:S(2)}) async-start(s8[7340032]{0:T(1024)(128)(4,1)} %bitcast.33), calls=%async_computation.18 | async-start | bytes 8388608
  200.2 8.2 %slice-start.9 = ((s8[7340032]{0:T(1024)(128)(4,1)}), s8[3145728]{0:T(1024)(128)(4,1)S(1)}, s32[]{:S(2)}) async-start(s8[7340032]{0:T(1024)(128)(4,1)} %bitcast.33), calls=%async_computation.19 | async-start | bytes 6291456
  208.4 11.8 %slice-start.4 = ((s8[14680064]{0:T(1024)(128)(4,1)}), s8[4194304]{0:T(1024)(128)(4,1)S(1)}, s32[]{:S(2)}) async-start(s8[14680064]{0:T(1024)(128)(4,1)} %bitcast.29), calls=%async_computation.14 | async-start | bytes 8388608
  208.4 11.8 %slice-start.5 = ((s8[14680064]{0:T(1024)(128)(4,1)}), s8[4194304]{0:T(1024)(128)(4,1)S(1)}, s32[]{:S(2)}) async-start(s8[14680064]{0:T(1024)(128)(4,1)} %bitcast.29), calls=%async_computation.15 | async-start | bytes 8388608
  212.5 7.7 %slice-start.6 = ((s8[14680064]{0:T(1024)(128)(4,1)}), s8[4194304]{0:T(1024)(128)(4,1)S(1)}, s32[]{:S(2)}) async-start(s8[14680064]{0:T(1024)(128)(4,1)} %bitcast.29), calls=%async_computation.16 | async-start | bytes 8388608
  212.5 7.7 %slice-start.7 = ((s8[14680064]{0:T(1024)(128)(4,1)}), s8[2097152]{0:T(1024)(128)(4,1)S(1)}, s32[]{:S(2)}) async-start(s8[14680064]{0:T(1024)(128)(4,1)} %bitcast.29), calls=%async_computation.17 | async-start | bytes 4194304
  232.0 232.4 %copy-start.1 = (bf16[8192,8]{0,1:T(8,128)(2,1)S(1)}, bf16[8192,8]{0,1:T(8,128)(2,1)}, u32[]{:S(2)}) copy-start(bf16[8192,8]{0,1:T(8,128)(2,1)} %param.8) | copy-start | bytes 393220
  232.1 184.6 %reduce-scatter.7.cloned.1.call-start = ((), (), s32[]{:S(2)}) async-start(), calls=%async_computation.6 | async-start | bytes 2621440 | tf_op jit(solution)/shard_map/reduce_scatter | solution.py:62
  281.0 181.2 %reduce-scatter.11.cloned.1.call-start = ((), (), s32[]{:S(2)}) async-start(), calls=%async_computation.9 | async-start | bytes 2621440 | tf_op jit(solution)/shard_map/reduce_scatter | solution.py:62
Sparse Core Ops, SparseCore 0:
  11.4 90.3 all-gather.2
  103.6 87.7 all-gather.4
  194.5 86.4 reduce-scatter.4
  284.2 86.4 reduce-scatter.8
  372.8 43.8 reduce-scatter.6
  418.9 43.1 reduce-scatter.10
